TPU v7x, 256 devices: a whole 4x4x8 slice. The times are simulated.
256 devices in a mesh: horiz: 64 (over x, z, core), depth: 4 (over y).
Axes of the slice: x: 4, y: 4, z: 8, core: 2. Of those that a mesh axis runs over, the one named last changes fastest.
Arguments:
- initial_state: float32 [4, 256, 8, 128], P(None, 'horiz', 'depth'), may hold values from 0 to 2
- explicit_blocks: float32 [256, 8, 4, 128, 128], P('horiz', 'depth'), may hold values from -0.0625 to 0.0625
- implicit_blocks: float32 [256, 8, 4, 128, 128], P('horiz', 'depth'), may hold values from -0.0625 to 0.0625
- pattern: int32 [256, 8, 4], P('horiz', 'depth'), may hold values from 0 to 24, as said below
- cavity_mask: int32 [256, 8, 128], P('horiz', 'depth'), may hold values 0 or 1
- melt_rate: float32 [256, 8, 128], P('horiz', 'depth'), may hold values from 0.2 to 2
- uptake_rate: float32 [256, 8, 128], P('horiz', 'depth'), may hold values from 0.2 to 2
Outputs:
- spun_up: float32 [4, 256, 8, 128], P(None, 'horiz', 'depth')
Inputs may be any that keep to these rules, and one draw needn't show every extreme that they name: `pattern`: code 5 (a + 2) + (b + 2) names the block a positions away horizontally and b in depth; the 4 codes of one block row differ.
All inputs are finite; a program needn't handle non-finite values. No bound on the sum of `cavity_mask` on one device may be relied on, other than what follows from the above.
Results may differ from a plain program's by a relative error of at most 0.0015.
Values sent between devices are 32-bit elements; how exact they have to be, the bound alone decides.
A program may use at most 64 MiB of HBM per device.

v0:
```python
import jax
import jax.numpy as jnp
from jax import lax
from jax.sharding import PartitionSpec as P

NEWTON = 2
KRYLOV = 3


time_step = 0.5
highest = lax.Precision.HIGHEST


def extended(value, sides, width):
    for axis, dim in sides:
        size, length = (lax.axis_size(axis), value.shape[dim])
        up = [(i, (i + 1) % size) for i in range(size - 1)]
        down = [(j, i) for i, j in up]
        last = lax.slice_in_dim(value, length - width, length, axis=dim)
        leading = lax.slice_in_dim(value, 0, width, axis=dim)
        before = lax.ppermute(last, axis, up)
        after = lax.ppermute(leading, axis, down)
        value = jnp.concatenate([before, value, after], axis=dim)
    return value


def one_hot_codes(pattern):
    return (pattern[..., None] == jnp.arange(25, dtype=jnp.int32)).astype(jnp.float32)


def block_product(padded, blocks, offset_codes):
    extent_horiz = offset_codes.shape[0]
    extent_depth = offset_codes.shape[1]
    shifted_views = [
        padded[
            :, offset // 5 : offset // 5 + extent_horiz, offset % 5 : offset % 5 + extent_depth, :
        ]
        for offset in range(25)
    ]
    stacked = jnp.stack(shifted_views)
    chosen = jnp.einsum("hdkc,cthdj->thdkj", offset_codes, stacked, precision=highest)
    return jnp.einsum("hdkij,thdkj->thdi", blocks, chosen, precision=highest)


def sources(tracers, forcing, uptake):
    iron_level = tracers[3]
    squared = iron_level * iron_level
    limitation = squared / (1.0 + squared)
    uptake_flux = uptake * tracers[1] * limitation
    return jnp.stack(
        [
            forcing * (1.0 - tracers[0]),
            -uptake_flux,
            0.5 * uptake_flux - 0.2 * tracers[2],
            forcing * tracers[0] - 0.05 * uptake_flux,
        ]
    )


def source_tangent(tracers, direction, forcing, uptake):
    iron_level = tracers[3]
    denominator = 1.0 + iron_level * iron_level
    limitation = iron_level * iron_level / denominator
    slope_term = 2.0 * iron_level / (denominator * denominator)
    flux_change = uptake * (direction[1] * limitation + tracers[1] * slope_term * direction[3])
    return jnp.stack(
        [
            -forcing * direction[0],
            -flux_change,
            0.5 * flux_change - 0.2 * direction[2],
            forcing * direction[0] - 0.05 * flux_change,
        ]
    )


def least_squares(hessenberg, start_norm):
    columns_count = hessenberg.shape[1]
    rotated = hessenberg
    target = jnp.zeros((columns_count + 1,), jnp.float32).at[0].set(start_norm)
    for column in range(columns_count):
        pivot_top = rotated[column, column]
        second = rotated[column + 1, column]
        radius = jnp.sqrt(pivot_top * pivot_top + second * second)
        cosine = pivot_top / radius
        sine_value = second / radius
        row_top = rotated[column]
        row_low = rotated[column + 1]
        rotated = (
            rotated.at[column]
            .set(cosine * row_top + sine_value * row_low)
            .at[column + 1]
            .set(cosine * row_low - sine_value * row_top)
        )
        target_top = target[column]
        target_low = target[column + 1]
        target = (
            target.at[column]
            .set(cosine * target_top + sine_value * target_low)
            .at[column + 1]
            .set(cosine * target_low - sine_value * target_top)
        )
    solution = jnp.zeros((columns_count,), jnp.float32)
    for column in reversed(range(columns_count)):
        partial_sum = target[column] - jnp.sum(
            rotated[column, column + 1 :] * solution[column + 1 :]
        )
        solution = solution.at[column].set(partial_sum / rotated[column, column])
    return solution


def per_device(
    initial_state, explicit_blocks, implicit_blocks, pattern, cavity_mask, melt_rate, uptake_rate
):
    offset_codes = one_hot_codes(pattern)
    forcing = cavity_mask.astype(jnp.float32) * melt_rate

    def explicit_ghosts(tracer_field):
        return extended(tracer_field, (("horiz", 1), ("depth", 2)), 2)

    def transport(tracer_field, padded_field, source_term):
        middle = (
            0.5 * tracer_field
            + block_product(padded_field, explicit_blocks, offset_codes)
            + time_step * source_term
        )
        padded_middle = extended(middle, (("horiz", 1), ("depth", 2)), 2)
        return middle + block_product(padded_middle, implicit_blocks, offset_codes)

    current = initial_state
    for newton_step in range(NEWTON):
        residual = current - transport(
            current, explicit_ghosts(current), sources(current, forcing, uptake_rate)
        )
        start_norm = jnp.sqrt(lax.psum(jnp.sum(residual * residual), ("horiz", "depth")))
        basis = [residual / start_norm]
        hessenberg = jnp.zeros((KRYLOV + 1, KRYLOV), jnp.float32)
        for column in range(KRYLOV):
            vector = basis[column]
            padded_vector = explicit_ghosts(vector)
            mapped = (
                transport(
                    vector, padded_vector, source_tangent(current, vector, forcing, uptake_rate)
                )
                - vector
            )
            product_list = []
            for earlier in range(column + 1):
                product = lax.psum(jnp.sum(basis[earlier] * mapped), ("horiz", "depth"))
                mapped = mapped - product * basis[earlier]
                product_list.append(product)
            products = jnp.stack(product_list)
            norm_value = jnp.sqrt(lax.psum(jnp.sum(mapped * mapped), ("horiz", "depth")))
            hessenberg = (
                hessenberg.at[: column + 1, column]
                .set(products)
                .at[column + 1, column]
                .set(norm_value)
            )
            if column + 1 < KRYLOV:
                basis.append(mapped / norm_value)
        weights = least_squares(hessenberg, start_norm)
        current = current + jnp.einsum(
            "n,ntabc->tabc", weights, jnp.stack(basis), precision=highest
        )
    return current


def solution(mesh):
    return jax.shard_map(
        per_device,
        mesh=mesh,
        in_specs=(
            P(None, "horiz", "depth", None),
            P("horiz", "depth", None, None, None),
            P("horiz", "depth", None, None, None),
            P("horiz", "depth", None),
            P("horiz", "depth", None),
            P("horiz", "depth", None),
            P("horiz", "depth", None),
        ),
        out_specs=P(None, "horiz", "depth", None),
        check_vma=False,
    )
```

profile of v0, /device:TPU:1, one launch (start us, length us, event | category | flops | bytes accessed | tf_op | source)
XLA Modules:
  0.0 1897.5 jit_solution(11349616918965531946)
XLA Ops:
  0.9 4.9 collective-permute-start
  12.1 4.0 collective-permute-start.2
  20.7 4.0 collective-permute-start.4
  29.8 4.1 collective-permute-start.6
  42.0 80.9 %psum.140 = f32[]{:T(128)} all-reduce(f32[]{:T(128)} %multiply_reduce_fusion.19), channel_id=1, replica_groups=mesh['horiz'=64,'depth'=4] {'horiz','depth'}, use_global_device_ids=true, to_apply=%region_1.0 | all-reduce | flops 1 | bytes 8 | tf_op jit(solution)/shard_map/psum | solution.py:134
  159.9 78.8 %psum.141 = f32[]{:T(128)} all-reduce(f32[]{:T(128)} %multiply_reduce_fusion.18), channel_id=1, replica_groups=mesh['horiz'=64,'depth'=4] {'horiz','depth'}, use_global_device_ids=true, to_apply=%region_3.0 | all-reduce | flops 1 | bytes 8 | tf_op jit(solution)/shard_map/psum | solution.py:148
  240.0 72.7 %psum.142 = f32[]{:T(128)} all-reduce(f32[]{:T(128)} %multiply_reduce_fusion.17), channel_id=1, replica_groups=mesh['horiz'=64,'depth'=4] {'horiz','depth'}, use_global_device_ids=true, to_apply=%region_5.0 | all-reduce | flops 1 | bytes 8 | tf_op jit(solution)/shard_map/psum | solution.py:152
  314.0 4.2 collective-permute-start.16
  346.1 3.6 collective-permute-done.23
  353.8 76.9 %psum.143 = f32[]{:T(128)} all-reduce(f32[]{:T(128)} %multiply_reduce_fusion.16), channel_id=1, replica_groups=mesh['horiz'=64,'depth'=4] {'horiz','depth'}, use_global_device_ids=true, to_apply=%region_8.0 | all-reduce | flops 1 | bytes 8 | tf_op jit(solution)/shard_map/psum | solution.py:148
  432.1 72.7 %psum.144 = f32[]{:T(128)} all-reduce(f32[]{:T(128)} %multiply_reduce_fusion.15), channel_id=1, replica_groups=mesh['horiz'=64,'depth'=4] {'horiz','depth'}, use_global_device_ids=true, to_apply=%region_10.0 | all-reduce | flops 1 | bytes 8 | tf_op jit(solution)/shard_map/psum | solution.py:148
  506.8 73.7 %psum.145 = f32[]{:T(128)} all-reduce(f32[]{:T(128)} %get-tuple-element.549), channel_id=1, replica_groups=mesh['horiz'=64,'depth'=4] {'horiz','depth'}, use_global_device_ids=true, to_apply=%region_12.0 | all-reduce | flops 1 | bytes 8 | tf_op jit(solution)/shard_map/psum | solution.py:152
  615.0 3.6 collective-permute-done.31
  623.7 77.8 %psum.146 = f32[]{:T(128)} all-reduce(f32[]{:T(128)} %get-tuple-element.545), channel_id=1, replica_groups=mesh['horiz'=64,'depth'=4] {'horiz','depth'}, use_global_device_ids=true, to_apply=%region_15.0 | all-reduce | flops 1 | bytes 8 | tf_op jit(solution)/shard_map/psum | solution.py:148
  704.2 73.1 %psum.147 = f32[]{:T(128)} all-reduce(f32[]{:T(128)} %multiply_reduce_fusion.12), channel_id=1, replica_groups=mesh['horiz'=64,'depth'=4] {'horiz','depth'}, use_global_device_ids=true, to_apply=%region_17.0 | all-reduce | flops 1 | bytes 8 | tf_op jit(solution)/shard_map/psum | solution.py:148
  779.3 73.7 %psum.148 = f32[]{:T(128)} all-reduce(f32[]{:T(128)} %multiply_reduce_fusion.11), channel_id=1, replica_groups=mesh['horiz'=64,'depth'=4] {'horiz','depth'}, use_global_device_ids=true, to_apply=%region_19.0 | all-reduce | flops 1 | bytes 8 | tf_op jit(solution)/shard_map/psum | solution.py:148
  855.5 73.5 %psum.149 = f32[]{:T(128)} all-reduce(f32[]{:T(128)} %multiply_reduce_fusion.10), channel_id=1, replica_groups=mesh['horiz'=64,'depth'=4] {'horiz','depth'}, use_global_device_ids=true, to_apply=%region_21.0 | all-reduce | flops 1 | bytes 8 | tf_op jit(solution)/shard_map/psum | solution.py:152
  929.7 3.9 broadcast_select_fusion.1
  952.4 4.2 collective-permute-start.32
  990.8 76.9 %psum.150 = f32[]{:T(128)} all-reduce(f32[]{:T(128)} %multiply_reduce_fusion.9), channel_id=1, replica_groups=mesh['horiz'=64,'depth'=4] {'horiz','depth'}, use_global_device_ids=true, to_apply=%region_24.0 | all-reduce | flops 1 | bytes 8 | tf_op jit(solution)/shard_map/psum | solution.py:134
  1104.8 78.3 %psum.151 = f32[]{:T(128)} all-reduce(f32[]{:T(128)} %multiply_reduce_fusion.8), channel_id=1, replica_groups=mesh['horiz'=64,'depth'=4] {'horiz','depth'}, use_global_device_ids=true, to_apply=%region_26.0 | all-reduce | flops 1 | bytes 8 | tf_op jit(solution)/shard_map/psum | solution.py:148
  1184.4 72.6 %psum.152 = f32[]{:T(128)} all-reduce(f32[]{:T(128)} %multiply_reduce_fusion.7), channel_id=1, replica_groups=mesh['horiz'=64,'depth'=4] {'horiz','depth'}, use_global_device_ids=true, to_apply=%region_28.0 | all-reduce | flops 1 | bytes 8 | tf_op jit(solution)/shard_map/psum | solution.py:152
  1258.3 4.2 collective-permute-start.48
  1290.0 3.6 collective-permute-done.55
  1297.1 76.9 %psum.153 = f32[]{:T(128)} all-reduce(f32[]{:T(128)} %multiply_reduce_fusion.6), channel_id=1, replica_groups=mesh['horiz'=64,'depth'=4] {'horiz','depth'}, use_global_device_ids=true, to_apply=%region_30.0 | all-reduce | flops 1 | bytes 8 | tf_op jit(solution)/shard_map/psum | solution.py:148
  1375.3 72.8 %psum.154 = f32[]{:T(128)} all-reduce(f32[]{:T(128)} %multiply_reduce_fusion.5), channel_id=1, replica_groups=mesh['horiz'=64,'depth'=4] {'horiz','depth'}, use_global_device_ids=true, to_apply=%region_32.0 | all-reduce | flops 1 | bytes 8 | tf_op jit(solution)/shard_map/psum | solution.py:148
  1450.0 73.7 %psum.155 = f32[]{:T(128)} all-reduce(f32[]{:T(128)} %get-tuple-element.537), channel_id=1, replica_groups=mesh['horiz'=64,'depth'=4] {'horiz','depth'}, use_global_device_ids=true, to_apply=%region_34.0 | all-reduce | flops 1 | bytes 8 | tf_op jit(solution)/shard_map/psum | solution.py:152
  1566.9 77.8 %psum.156 = f32[]{:T(128)} all-reduce(f32[]{:T(128)} %get-tuple-element.533), channel_id=1, replica_groups=mesh['horiz'=64,'depth'=4] {'horiz','depth'}, use_global_device_ids=true, to_apply=%region_36.0 | all-reduce | flops 1 | bytes 8 | tf_op jit(solution)/shard_map/psum | solution.py:148
  1647.4 72.6 %psum.157 = f32[]{:T(128)} all-reduce(f32[]{:T(128)} %multiply_reduce_fusion.2), channel_id=1, replica_groups=mesh['horiz'=64,'depth'=4] {'horiz','depth'}, use_global_device_ids=true, to_apply=%region_38.0 | all-reduce | flops 1 | bytes 8 | tf_op jit(solution)/shard_map/psum | solution.py:148
  1722.1 74.1 %psum.158 = f32[]{:T(128)} all-reduce(f32[]{:T(128)} %multiply_reduce_fusion.1), channel_id=1, replica_groups=mesh['horiz'=64,'depth'=4] {'horiz','depth'}, use_global_device_ids=true, to_apply=%region_40.0 | all-reduce | flops 1 | bytes 8 | tf_op jit(solution)/shard_map/psum | solution.py:148
  1798.7 73.5 %psum.159 = f32[]{:T(128)} all-reduce(f32[]{:T(128)} %multiply_reduce_fusion), channel_id=1, replica_groups=mesh['horiz'=64,'depth'=4] {'horiz','depth'}, use_global_device_ids=true, to_apply=%region_42.0 | all-reduce | flops 1 | bytes 8 | tf_op jit(solution)/shard_map/psum | solution.py:152
  1872.9 3.9 broadcast_select_fusion
  (711 shorter events, 311.1 us)
Async XLA Ops:
  0.9 8.3 collective-permute-start
  5.8 5.0 collective-permute-start.1
  10.8 5.3 collective-permute-start.3
  12.1 5.0 collective-permute-start.2
  20.7 5.9 collective-permute-start.4
  24.8 5.0 collective-permute-start.5
  29.8 5.4 collective-permute-start.6
  126.3 5.0 collective-permute-start.9
  140.3 5.5 collective-permute-start.12
  143.9 5.0 collective-permute-start.13
  314.0 6.2 collective-permute-start.16
  318.3 5.0 collective-permute-start.17
  333.4 5.3 collective-permute-start.20
  336.8 5.0 collective-permute-start.21
  581.1 5.4 collective-permute-start.24
  584.5 5.0 collective-permute-start.25
  599.9 7.8 collective-permute-start.28
  603.2 5.0 collective-permute-start.29
  608.2 6.8 collective-permute-start.30
  952.4 6.2 collective-permute-start.32
  956.6 5.0 collective-permute-start.33
  971.7 5.3 collective-permute-start.36
  975.1 5.0 collective-permute-start.37
  1071.2 5.0 collective-permute-start.41
  1085.0 5.2 collective-permute-start.44
  1088.3 5.0 collective-permute-start.45
  1258.3 6.2 collective-permute-start.48
  1262.6 5.0 collective-permute-start.49
  1278.0 5.3 collective-permute-start.52
  1524.3 5.4 collective-permute-start.56
  1543.0 6.1 collective-permute-start.60
  1551.4 7.0 collective-permute-start.62
  (43 other events, 439.1 us)
where the time goes:
time: 1910 us; the launch traced here: 1900 us
  blocking collectives  1500 us (79%)
  starting transfers between devices  152 us (8%)
  waiting for transfers between devices  94.7 us (5%)
  other arithmetic  47.3 us (2%)
  matrix products  42 us (2%)
  between operations  35 us (2%)
  local copies, waits for them, and re-layouts  23.5 us (1%)
    psum x12, blocking collectives, per_device(): product = lax.psum(jnp.sum(basis[earlier] * mapped), ('horiz', 'depth'))  906 us
    psum x6, blocking collectives, per_device(): lax.psum(jnp.sum(mapped * mapped), ('horiz', 'depth'))  440 us
    psum x2, blocking collectives, per_device(): lax.psum(jnp.sum(residual * residual), ('horiz', 'depth'))  158 us
    ppermute x32, starting transfers between devices, extended(): before = lax.ppermute(last, axis, up)  99.5 us
    ppermute x32, waiting for transfers between devices, extended(): after = lax.ppermute(leading, axis, down)  93.7 us
    ppermute x32, starting transfers between devices, extended(): after = lax.ppermute(leading, axis, down)  52.4 us
  transfers between devices with their start and end apart: 64, of which 32 were waited for; matrix products, arithmetic and copies ran while one was open for 1% of the time, Pallas kernels for 0%

commit v1 on v0

v1 whole, which is shorter than its diff:
```python
import functools
import jax
import jax.numpy as jnp
from jax import lax
from jax.experimental import pallas as pl
from jax.experimental.pallas import tpu as pltpu
from jax.sharding import PartitionSpec as P

NEWTON = 2
KRYLOV = 3
SHIFT = 0.4

f32 = jnp.float32
bf16 = jnp.bfloat16
MESH = pl.DeviceIdType.MESH

SLOT = 192
OWN = 80
UPTAKE = 15
SLOTS = 16
ZERO = SLOTS * SLOT

DIRECTIONS = [(sh, sd) for sd in (-1, 0, 1) for sh in (-1, 0, 1) if (sh, sd) != (0, 0)]


def rows(start, size):
    return pl.ds(pl.multiple_of(start, 16) if not isinstance(start, int) else start, size)


def kernel(
    nh, nd, ga, c_in, a_hbm, b_hbm, pat, mask, melt, upt, out,
    X, GB, IDX, st_a, st_b, WA, WB, PR, FU, K, RA, RB,
    w_sem, r_sem, s_sem, ra_sem, rb_sem, rs_sem,
):
    gb = (nh // ga) * nd
    h = lax.axis_index("horiz")
    d = lax.axis_index("depth")

    copy_a = pltpu.make_async_copy(a_hbm, st_a, w_sem.at[0])
    copy_b = pltpu.make_async_copy(b_hbm, st_b, w_sem.at[1])
    copy_a.start()
    copy_b.start()

    h_hi = h // ga
    h_lo = lax.rem(h, ga)
    index_b = h_hi * nd + d

    def neighbour(sh, sd):
        return (lax.rem(h + sh + nh, nh), lax.rem(d + sd + nd, nd))

    def partner_a(k):
        return (h_hi * ga + lax.rem(h_lo + k, ga), d)

    def partner_b(k):
        index = lax.rem(index_b + k, gb)
        return ((index // nd) * ga + h_lo, lax.rem(index, nd))

    barrier = pltpu.get_barrier_semaphore()
    for sh, sd in DIRECTIONS:
        pl.semaphore_signal(barrier, inc=1, device_id=neighbour(sh, sd), device_id_type=MESH)

    def greet_a(k, _):
        pl.semaphore_signal(barrier, inc=1, device_id=partner_a(k), device_id_type=MESH)
        return 0

    def greet_b(k, _):
        pl.semaphore_signal(barrier, inc=1, device_id=partner_b(k), device_id_type=MESH)
        return 0

    lax.fori_loop(1, ga, greet_a, 0)
    lax.fori_loop(1, gb, greet_b, 0)

    for hh in range(4):
        for dd in range(2):
            o = hh * 2 + dd
            for t in range(4):
                X[pl.ds(OWN + o * 4 + t, 1), :] = c_in[t, hh, pl.ds(dd, 1), :]
            u_row = upt[hh, pl.ds(dd, 1), :]
            X[pl.ds(UPTAKE * SLOT + OWN + o * 4, 4), :] = jnp.broadcast_to(u_row, (4, 128))
            FU[pl.ds(o, 1), :] = mask[hh, pl.ds(dd, 1), :].astype(f32) * melt[hh, pl.ds(dd, 1), :]
            FU[pl.ds(8 + o, 1), :] = u_row
    X[pl.ds(ZERO, 32), :] = jnp.zeros((32, 128), f32)

    for o in range(8):
        for k in range(4):
            code = pat[o // 2, o % 2, k]
            five = lax.div(code, 5)
            row = (o // 2) + five
            dep = (o % 2) + code - 5 * five
            band = lax.div(dep, 2)
            IDX[o * 4 + k] = band * 16 + row * 2 + dep - 2 * band

    pl.semaphore_wait(barrier, 8 + (ga - 1) + (gb - 1))

    starts = []
    for sh, sd in DIRECTIONS:
        n_rows = 16 if sh else 32
        src_h = {1: 4, -1: 2, 0: 2}[sh]
        dst_h = {1: 0, -1: 6, 0: 2}[sh]
        inside = jnp.logical_and(
            jnp.logical_and(h + sh >= 0, h + sh < nh), jnp.logical_and(d + sd >= 0, d + sd < nd)
        )
        starts.append(
            (inside, (16 + src_h * 2) * 4, ((1 - sd) * 16 + dst_h * 2) * 4, n_rows, neighbour(sh, sd))
        )

    def exchange(slot):
        base = slot * SLOT
        for inside, src, dst, n_rows, target in starts:
            pltpu.make_async_remote_copy(
                src_ref=X.at[rows(jnp.where(inside, base + src, ZERO), n_rows)],
                dst_ref=X.at[rows(base + dst, n_rows)],
                send_sem=s_sem.at[slot],
                recv_sem=r_sem.at[slot],
                device_id=target,
                device_id_type=MESH,
            ).start()

    def arrived(slot, sem):
        span = X.at[rows(slot * SLOT, SLOT - 32)]
        pltpu.make_async_copy(span, span, sem.at[slot]).wait()

    def own(slot):
        return [X[pl.ds(slot * SLOT + OWN + t, 8, stride=4), :] for t in range(4)]

    def set_own(slot, value):
        for t in range(4):
            X[pl.ds(slot * SLOT + OWN + t, 8, stride=4), :] = value[t]

    def split_blocks(stage, weights):
        def body(o, _):
            for k in range(4):
                block = stage[o // 2, lax.rem(o, 2), k]
                high = block.astype(bf16)
                weights[o, pl.ds(0, 128), pl.ds(k * 128, 128)] = high
                weights[o, pl.ds(128, 128), pl.ds(k * 128, 128)] = (block - high.astype(f32)).astype(bf16)
            return 0

        lax.fori_loop(0, 8, body, 0)

    upper = lax.broadcasted_iota(jnp.int32, (8, 128), 0) < 4

    def product(slot, weights):
        for pair in range(24):
            x = X[pl.ds(pl.multiple_of(slot * SLOT + pair * 8, 8), 8), :]
            high = x.astype(bf16).astype(f32)
            low = pltpu.roll(x - high, 4, axis=0)
            GB[2 * pair] = jnp.where(upper, high, low)
            GB[2 * pair + 1] = jnp.where(upper, low, high)
        for pair in range(4):
            sums = []
            for o in (2 * pair, 2 * pair + 1):
                lhs = jnp.concatenate(
                    [
                        GB[IDX[o * 4 + k]].astype(bf16)
                        for k in range(4)
                    ],
                    axis=1,
                )
                both = lax.dot_general(
                    lhs, weights[o], (((1,), (1,)), ((), ())), preferred_element_type=f32
                )
                both = both[:, :128] + both[:, 128:]
                sums.append(both + pltpu.roll(both, 4, axis=0))
            PR[pl.ds(pair * 8, 8), :] = jnp.where(upper, sums[0], sums[1])
        return [PR[pl.ds(t, 8, stride=4), :] for t in range(4)]

    def all_sum(step, row):
        RA[step, h_lo] = row

        def send_a(k, _):
            pltpu.make_async_remote_copy(
                src_ref=RA.at[step, h_lo], dst_ref=RA.at[step, h_lo],
                send_sem=rs_sem.at[2 * step], recv_sem=ra_sem.at[step],
                device_id=partner_a(k), device_id_type=MESH,
            ).start()
            return 0

        lax.fori_loop(1, ga, send_a, 0)
        span = RA.at[step, pl.ds(0, ga - 1)]
        pltpu.make_async_copy(span, span, ra_sem.at[step]).wait()
        RB[step, index_b] = jnp.sum(RA[step], axis=0)

        def send_b(k, _):
            pltpu.make_async_remote_copy(
                src_ref=RB.at[step, index_b], dst_ref=RB.at[step, index_b],
                send_sem=rs_sem.at[2 * step + 1], recv_sem=rb_sem.at[step],
                device_id=partner_b(k), device_id_type=MESH,
            ).start()
            return 0

        lax.fori_loop(1, gb, send_b, 0)
        span = RB.at[step, pl.ds(0, gb - 1)]
        pltpu.make_async_copy(span, span, rb_sem.at[step]).wait()
        return jnp.sum(RB[step], axis=0)

    lane = lax.broadcasted_iota(jnp.int32, (1, 128), 1)

    def coefficients(step):
        vectors = [[K[j * 4 + t] for t in range(4)] for j in range(4)]
        pairs = [(i, j) for i in range(4) for j in range(i, 4)]
        row = jnp.zeros((1, 128), f32)
        for number, (i, j) in enumerate(pairs):
            part = sum(vectors[i][t] * vectors[j][t] for t in range(4))
            total = jnp.sum(jnp.sum(part, axis=0, keepdims=True), axis=1, keepdims=True)
            row = jnp.where(lane == number, total, row)
        total = all_sum(step, row)
        gram = {
            pair: jnp.sum(jnp.where(lane == number, total, 0.0), axis=1, keepdims=True)
            for number, pair in enumerate(pairs)
        }
        zero = jnp.zeros((1, 1), f32)
        R = [[zero] * 4 for _ in range(4)]
        for i in range(4):
            pivot = gram[i, i]
            for m in range(i):
                pivot = pivot - R[m][i] * R[m][i]
            pivot = jnp.maximum(pivot, 1e-14 * gram[i, i])
            R[i][i] = jnp.sqrt(pivot)
            inverse = 1.0 / R[i][i]
            for j in range(i + 1, 4):
                value = gram[i, j]
                for m in range(i):
                    value = value - R[m][i] * R[m][j]
                R[i][j] = value * inverse
        hess = [[(SHIFT - 1.0) * R[i][j] + R[i][j + 1] for j in range(3)] for i in range(4)]
        target = [R[0][0], zero, zero, zero]
        for c in range(3):
            top, low = hess[c][c], hess[c + 1][c]
            inverse = 1.0 / jnp.sqrt(top * top + low * low)
            cosine, sine = top * inverse, low * inverse
            for j in range(c, 3):
                top, low = hess[c][j], hess[c + 1][j]
                hess[c][j] = cosine * top + sine * low
                hess[c + 1][j] = cosine * low - sine * top
            top, low = target[c], target[c + 1]
            target[c] = cosine * top + sine * low
            target[c + 1] = cosine * low - sine * top
        answer = [zero] * 3
        for c in (2, 1, 0):
            value = target[c]
            for j in range(c + 1, 3):
                value = value - hess[c][j] * answer[j]
            answer[c] = value / hess[c][c]
        return answer

    def limitation(iron):
        squared = iron * iron
        return squared / (1.0 + squared)

    def slope(iron):
        denominator = 1.0 + iron * iron
        return 2.0 * iron / (denominator * denominator)

    def krylov(first, c, residual):
        forcing, uptake = FU[pl.ds(0, 8), :], FU[pl.ds(8, 8), :]
        flux_one = uptake * limitation(c[3])
        flux_three = uptake * c[1] * slope(c[3])
        for t in range(4):
            K[t] = residual[t]

        def step(j, _):
            v = [K[4 * j + t] for t in range(4)]
            slot = first + 2 * j
            set_own(slot, v)
            exchange(slot)
            change = flux_one * v[1] + flux_three * v[3]
            middle = [
                0.5 * v[0] - 0.5 * forcing * v[0],
                0.5 * v[1] - 0.5 * change,
                0.4 * v[2] + 0.25 * change,
                0.5 * v[3] + 0.5 * forcing * v[0] - 0.025 * change,
            ]
            arrived(slot, r_sem)
            image = product(slot, WA)
            middle = [m + i for m, i in zip(middle, image)]
            set_own(slot + 1, middle)
            exchange(slot + 1)
            arrived(slot + 1, r_sem)
            image = product(slot + 1, WB)
            for t in range(4):
                K[4 * (j + 1) + t] = middle[t] + image[t] - SHIFT * v[t]
            return 0

        lax.fori_loop(0, KRYLOV, step, 0)

    exchange(0)
    exchange(UPTAKE)
    copy_a.wait()
    split_blocks(st_a, WA)
    arrived(0, r_sem)
    image = product(0, WA)
    c = own(0)
    forcing, uptake = FU[pl.ds(0, 8), :], FU[pl.ds(8, 8), :]
    flux = uptake * c[1] * limitation(c[3])
    source = [
        forcing * (1.0 - c[0]),
        -flux,
        0.5 * flux - 0.2 * c[2],
        forcing * c[0] - 0.05 * flux,
    ]
    middle = [0.5 * c[t] + image[t] + 0.5 * source[t] for t in range(4)]
    set_own(1, middle)
    exchange(1)
    copy_b.wait()
    split_blocks(st_b, WB)
    arrived(1, r_sem)
    image = product(1, WB)
    krylov(2, c, [c[t] - middle[t] - image[t] for t in range(4)])
    weights = coefficients(0)

    arrived(UPTAKE, r_sem)

    def wide(slot, t):
        return X[pl.ds(slot * SLOT + t, 48, stride=4), :]

    def wide_sum(first_slot, t):
        return sum(weights[j] * wide(first_slot + 2 * j, t) for j in range(3))

    tracer_old, iron_old = wide(0, 1), wide(0, 3)
    iron_step = wide_sum(2, 3)
    tracer_new, iron_new = tracer_old + wide_sum(2, 1), iron_old + iron_step
    rest = wide(UPTAKE, 0) * (
        tracer_new * (limitation(iron_new) - limitation(iron_old)) - tracer_old * slope(iron_old) * iron_step
    )
    for t in range(4):
        value = wide(1, t) + wide_sum(3, t)
        if t:
            value = value + (0.0, -0.5, 0.25, -0.025)[t] * rest
        X[pl.ds(8 * SLOT + t, 48, stride=4), :] = value
    image = product(8, WB)
    middle = own(8)
    c = [own(0)[t] + sum(weights[j] * K[4 * j + t] for j in range(3)) for t in range(4)]

    krylov(9, c, [c[t] - middle[t] - image[t] for t in range(4)])
    weights = coefficients(1)
    for t in range(4):
        out[pl.ds(t, 8, stride=4), :] = c[t] + sum(weights[j] * K[4 * j + t] for j in range(3))

    for slot in (0, 1, 2, 3, 4, 5, 6, 7, 9, 10, 11, 12, 13, 14, UPTAKE):
        arrived(slot, s_sem)
    for step in range(NEWTON):
        span = RA.at[step, pl.ds(0, ga - 1)]
        pltpu.make_async_copy(span, span, rs_sem.at[2 * step]).wait()
        span = RB.at[step, pl.ds(0, gb - 1)]
        pltpu.make_async_copy(span, span, rs_sem.at[2 * step + 1]).wait()


def per_device(nh, nd, state, explicit_blocks, implicit_blocks, pattern, cavity_mask, melt_rate, uptake_rate):
    ga = 16 if nh % 16 == 0 else 2
    gb = (nh // ga) * nd
    vmem = pl.BlockSpec(memory_space=pltpu.VMEM)
    result = pl.pallas_call(
        functools.partial(kernel, nh, nd, ga),
        out_shape=jax.ShapeDtypeStruct((32, 128), f32),
        in_specs=[
            vmem,
            pl.BlockSpec(memory_space=pl.ANY),
            pl.BlockSpec(memory_space=pl.ANY),
            pl.BlockSpec(memory_space=pltpu.SMEM),
            vmem,
            vmem,
            vmem,
        ],
        out_specs=vmem,
        scratch_shapes=[
            pltpu.VMEM((SLOTS * SLOT + 32, 128), f32),
            pltpu.VMEM((48, 8, 128), f32),
            pltpu.SMEM((32,), jnp.int32),
            pltpu.VMEM((4, 2, 4, 128, 128), f32),
            pltpu.VMEM((4, 2, 4, 128, 128), f32),
            pltpu.VMEM((8, 256, 512), bf16),
            pltpu.VMEM((8, 256, 512), bf16),
            pltpu.VMEM((32, 128), f32),
            pltpu.VMEM((16, 128), f32),
            pltpu.VMEM((16, 8, 128), f32),
            pltpu.VMEM((NEWTON, ga, 1, 128), f32),
            pltpu.VMEM((NEWTON, gb, 1, 128), f32),
            pltpu.SemaphoreType.DMA((2,)),
            pltpu.SemaphoreType.DMA((SLOTS,)),
            pltpu.SemaphoreType.DMA((SLOTS,)),
            pltpu.SemaphoreType.DMA((NEWTON,)),
            pltpu.SemaphoreType.DMA((NEWTON,)),
            pltpu.SemaphoreType.DMA((2 * NEWTON,)),
        ],
        compiler_params=pltpu.CompilerParams(
            collective_id=0, has_side_effects=True, vmem_limit_bytes=24 * 1024 * 1024
        ),
    )(state, explicit_blocks, implicit_blocks, pattern, cavity_mask, melt_rate, uptake_rate)
    return result.reshape(4, 2, 4, 128).transpose(2, 0, 1, 3)


def solution(mesh):
    nh, nd = mesh.shape["horiz"], mesh.shape["depth"]
    return jax.shard_map(
        functools.partial(per_device, nh, nd),
        mesh=mesh,
        in_specs=(
            P(None, "horiz", "depth", None),
            P("horiz", "depth", None, None, None),
            P("horiz", "depth", None, None, None),
            P("horiz", "depth", None),
            P("horiz", "depth", None),
            P("horiz", "depth", None),
            P("horiz", "depth", None),
        ),
        out_specs=P(None, "horiz", "depth", None),
        check_vma=False,
    )
```

time: 1910 us -> 113 us (0.06)
  blocking collectives: 1500 us -> 0 us
  starting transfers between devices: 152 us -> 0 us
  Pallas kernels: 0 us -> 106 us
  waiting for transfers between devices: 94.7 us -> 0 us
  other arithmetic: 47.3 us -> 0 us
  matrix products: 42 us -> 0 us
  between operations: 35 us -> 0.02 us
    psum x20 -> x0, blocking collectives: 1500 us -> none  [the longest x12 906 us: per_device(): product = lax.psum(jnp.sum(basis[earlier] * mapped), ('horiz', 'depth'))]
    ppermute x64 -> x0, starting transfers between devices: 152 us -> none  [the longest x32 99.5 us: extended(): before = lax.ppermute(last, axis, up)]
    pallas_call x0 -> x1, Pallas kernels: none -> 106 us  [per_device(): pl.pallas_call(functools.partial(kernel, nh, nd, ga), out_shape=jax.Shape...]
    ppermute x64 -> x0, waiting for transfers between devices: 94.7 us -> none  [the longest x32 93.7 us: extended(): after = lax.ppermute(leading, axis, down)]
    dot_general x34 -> x0, matrix products: 42 us -> none  [the longest x16 32.3 us: block_product(): return jnp.einsum('hdkij,thdkj->thdi', blocks, chosen, precision=highest)]
    reduce_sum x22 -> x0, other arithmetic: 27 us -> none  [the longest x12 12.9 us: per_device(): product = lax.psum(jnp.sum(basis[earlier] * mapped), ('horiz', 'depth'))]
  transfers between devices with their start and end apart: 64 -> 0, of which waited for: 32 -> 0; matrix products, arithmetic and copies ran while one was open for 1% -> 0% of each run, Pallas kernels for 0% -> 0%
where the time goes in v1:
time: 113 us
  Pallas kernels  106 us (94%)
  local copies, waits for them, and re-layouts  7.26 us (6%)
    pallas_call x1, Pallas kernels, per_device(): pl.pallas_call(functools.partial(kernel, nh, nd, ga), out_shape=jax.Shape...  106 us
    unnamed x14, local copies, waits for them, and re-layouts  6.64 us

profile of v1, /device:TPU:1, one launch (start us, length us, event | category | flops | bytes accessed | tf_op | source)
XLA Modules:
  0.0 112.9 jit_solution(642587096849210082)
XLA Ops:
  0.0 0.0 copy-start
  0.0 1.6 %copy-done = f32[4,2,4,128,128]{4,3,2,1,0:T(8,128)S(1)} copy-done((f32[4,2,4,128,128]{4,3,2,1,0:T(8,128)S(1)}, f32[4,2,4,128,128]{4,3,2,1,0:T(8,128)}, u32[]{:S(2)}) %copy-start) | copy-done | bytes 2097176
  1.6 0.0 copy-start.1
  1.6 1.6 %copy-done.1 = f32[4,2,4,128,128]{4,3,2,1,0:T(8,128)S(1)} copy-done((f32[4,2,4,128,128]{4,3,2,1,0:T(8,128)S(1)}, f32[4,2,4,128,128]{4,3,2,1,0:T(8,128)}, u32[]{:S(2)}) %copy-start.1) | copy-done | bytes 2097176
  3.2 0.0 copy-start.2
  3.2 0.7 copy-done.2
  3.9 0.0 copy-start.3
  3.9 0.7 copy-done.3
  4.6 0.0 copy-start.4
  4.6 0.7 copy-done.4
  5.3 0.0 copy-start.5
  5.3 0.7 copy-done.5
  6.0 0.0 copy-start.6
  6.0 0.7 copy-done.6
  6.7 105.7 %shard_map.73 = f32[32,128]{1,0:T(8,128)S(1)} custom-call(f32[4,4,2,128]{3,2,1,0:T(2,128)S(1)} %copy-done.2, f32[4,2,4,128,128]{4,3,2,1,0:T(8,128)S(1)} %copy-done, f32[4,2,4,128,128]{4,3,2,1,0:T(8,128)S(1)} %copy-done.1, s32[4,2,4]{2,1,0:T(2,128)S(1)} %copy-done.3, s32[4,2,128]{2,1,0:T(2,128)S(1)} %copy-done.4, f32[4,2,128]{2,1,0:T(2,128)S(1)} %copy-done.5, ...), custom_call_target="tpu_custom_call" | custom-call | tf_op jit(solution)/shard_map/pallas_call | solution.py:353
  112.3 0.6 copy.10
Async XLA Ops:
  0.0 1.6 %copy-start = (f32[4,2,4,128,128]{4,3,2,1,0:T(8,128)S(1)}, f32[4,2,4,128,128]{4,3,2,1,0:T(8,128)}, u32[]{:S(2)}) copy-start(f32[4,2,4,128,128]{4,3,2,1,0:T(8,128)} %a_hbm.1) | copy-start | bytes 6291460
  1.6 1.6 %copy-start.1 = (f32[4,2,4,128,128]{4,3,2,1,0:T(8,128)S(1)}, f32[4,2,4,128,128]{4,3,2,1,0:T(8,128)}, u32[]{:S(2)}) copy-start(f32[4,2,4,128,128]{4,3,2,1,0:T(8,128)} %b_hbm.1) | copy-start | bytes 6291460
  3.2 0.7 copy-start.2
  3.9 0.7 copy-start.3
  4.6 0.7 copy-start.4
  5.3 0.7 copy-start.5
  6.0 0.7 copy-start.6

commit v2 on v1

--- a/solution.py
+++ b/solution.py
@@ -8,7 +8,7 @@
 
 NEWTON = 2
 KRYLOV = 3
-SHIFT = 0.4
+SHIFT = 0.3
 
 f32 = jnp.float32
 bf16 = jnp.bfloat16
@@ -20,7 +20,7 @@
 SLOTS = 16
 ZERO = SLOTS * SLOT
 
-DIRECTIONS = [(sh, sd) for sd in (-1, 0, 1) for sh in (-1, 0, 1) if (sh, sd) != (0, 0)]
+DIRECTIONS = [(1, 1), (-1, 1), (1, -1), (-1, -1), (0, 1), (0, -1), (1, 0), (-1, 0)]
 
 
 def rows(start, size):
@@ -28,14 +28,22 @@
 
 
 def kernel(
-    nh, nd, ga, c_in, a_hbm, b_hbm, pat, mask, melt, upt, out,
-    X, GB, IDX, st_a, st_b, WA, WB, PR, FU, K, RA, RB,
+    nh, nd, ga, c_hbm, a_hbm, b_hbm, pat_hbm, mask_hbm, melt_hbm, upt_hbm, out,
+    c_in, pat, mask, melt, upt, X, GB, IDX, st_a, st_b, WA, WB, PR, FU, K, RA, RB,
     w_sem, r_sem, s_sem, ra_sem, rb_sem, rs_sem,
 ):
     gb = (nh // ga) * nd
     h = lax.axis_index("horiz")
     d = lax.axis_index("depth")
 
+    small = [
+        pltpu.make_async_copy(source, target, w_sem.at[2 + number])
+        for number, (source, target) in enumerate(
+            [(c_hbm, c_in), (upt_hbm, upt), (pat_hbm, pat), (mask_hbm, mask), (melt_hbm, melt)]
+        )
+    ]
+    for copy in small:
+        copy.start()
     copy_a = pltpu.make_async_copy(a_hbm, st_a, w_sem.at[0])
     copy_b = pltpu.make_async_copy(b_hbm, st_b, w_sem.at[1])
     copy_a.start()
@@ -45,8 +53,27 @@
     h_lo = lax.rem(h, ga)
     index_b = h_hi * nd + d
 
-    def neighbour(sh, sd):
-        return (lax.rem(h + sh + nh, nh), lax.rem(d + sd + nd, nd))
+    sends = []
+    for sh, sd in DIRECTIONS:
+        n_rows = 16 if sh else 32
+        src_h = {1: 4, -1: 2, 0: 2}[sh]
+        dst_h = {1: 0, -1: 6, 0: 2}[sh]
+        in_h = jnp.logical_and(h + sh >= 0, h + sh < nh)
+        in_d = jnp.logical_and(d + sd >= 0, d + sd < nd)
+        other_d = d + 1 - 2 * lax.rem(d, 2)
+        other_h = h + 1 - 2 * lax.rem(h, 2)
+        near_h = h + sh if sh else other_h
+        target = (
+            jnp.where(in_h, jnp.where(in_d, h + sh, near_h), h),
+            jnp.where(in_h, jnp.where(in_d, d + sd, d), other_d),
+        )
+        far_h = {1: 6, -1: 0, 0: 2}[sh]
+        position = jnp.where(
+            in_h,
+            jnp.where(in_d, (1 - sd) * 16 + dst_h * 2, (1 + sd) * 16 + dst_h * 2),
+            (1 - sd) * 16 + far_h * 2,
+        )
+        sends.append((jnp.logical_and(in_h, in_d), (16 + src_h * 2) * 4, position * 4, n_rows, target))
 
     def partner_a(k):
         return (h_hi * ga + lax.rem(h_lo + k, ga), d)
@@ -56,8 +83,8 @@
         return ((index // nd) * ga + h_lo, lax.rem(index, nd))
 
     barrier = pltpu.get_barrier_semaphore()
-    for sh, sd in DIRECTIONS:
-        pl.semaphore_signal(barrier, inc=1, device_id=neighbour(sh, sd), device_id_type=MESH)
+    for *_, target in sends:
+        pl.semaphore_signal(barrier, inc=1, device_id=target, device_id_type=MESH)
 
     def greet_a(k, _):
         pl.semaphore_signal(barrier, inc=1, device_id=partner_a(k), device_id_type=MESH)
@@ -70,6 +97,8 @@
     lax.fori_loop(1, ga, greet_a, 0)
     lax.fori_loop(1, gb, greet_b, 0)
 
+    for copy in small:
+        copy.wait()
     for hh in range(4):
         for dd in range(2):
             o = hh * 2 + dd
@@ -92,21 +121,9 @@
 
     pl.semaphore_wait(barrier, 8 + (ga - 1) + (gb - 1))
 
-    starts = []
-    for sh, sd in DIRECTIONS:
-        n_rows = 16 if sh else 32
-        src_h = {1: 4, -1: 2, 0: 2}[sh]
-        dst_h = {1: 0, -1: 6, 0: 2}[sh]
-        inside = jnp.logical_and(
-            jnp.logical_and(h + sh >= 0, h + sh < nh), jnp.logical_and(d + sd >= 0, d + sd < nd)
-        )
-        starts.append(
-            (inside, (16 + src_h * 2) * 4, ((1 - sd) * 16 + dst_h * 2) * 4, n_rows, neighbour(sh, sd))
-        )
-
     def exchange(slot):
         base = slot * SLOT
-        for inside, src, dst, n_rows, target in starts:
+        for inside, src, dst, n_rows, target in sends:
             pltpu.make_async_remote_copy(
                 src_ref=X.at[rows(jnp.where(inside, base + src, ZERO), n_rows)],
                 dst_ref=X.at[rows(base + dst, n_rows)],
@@ -353,17 +370,14 @@
     result = pl.pallas_call(
         functools.partial(kernel, nh, nd, ga),
         out_shape=jax.ShapeDtypeStruct((32, 128), f32),
-        in_specs=[
-            vmem,
-            pl.BlockSpec(memory_space=pl.ANY),
-            pl.BlockSpec(memory_space=pl.ANY),
-            pl.BlockSpec(memory_space=pltpu.SMEM),
-            vmem,
-            vmem,
-            vmem,
-        ],
+        in_specs=[pl.BlockSpec(memory_space=pltpu.HBM)] * 7,
         out_specs=vmem,
         scratch_shapes=[
+            pltpu.VMEM((4, 4, 2, 128), f32),
+            pltpu.SMEM((4, 2, 4), jnp.int32),
+            pltpu.VMEM((4, 2, 128), jnp.int32),
+            pltpu.VMEM((4, 2, 128), f32),
+            pltpu.VMEM((4, 2, 128), f32),
             pltpu.VMEM((SLOTS * SLOT + 32, 128), f32),
             pltpu.VMEM((48, 8, 128), f32),
             pltpu.SMEM((32,), jnp.int32),
@@ -376,7 +390,7 @@
             pltpu.VMEM((16, 8, 128), f32),
             pltpu.VMEM((NEWTON, ga, 1, 128), f32),
             pltpu.VMEM((NEWTON, gb, 1, 128), f32),
-            pltpu.SemaphoreType.DMA((2,)),
+            pltpu.SemaphoreType.DMA((7,)),
             pltpu.SemaphoreType.DMA((SLOTS,)),
             pltpu.SemaphoreType.DMA((SLOTS,)),
             pltpu.SemaphoreType.DMA((NEWTON,)),

time: 113 us -> 97.5 us (0.86)
  Pallas kernels: 106 us -> 89.9 us
    pallas_call x1, Pallas kernels: 106 us -> 89.9 us  [per_device(): pl.pallas_call(functools.partial(kernel, nh, nd, ga), out_shape=jax.Shape...]
where the time goes in v2:
time: 97.5 us; the launch traced here: 97.2 us
  Pallas kernels  89.9 us (92%)
  local copies, waits for them, and re-layouts  7.26 us (7%)
    pallas_call x1, Pallas kernels, per_device(): pl.pallas_call(functools.partial(kernel, nh, nd, ga), out_shape=jax.Shape...  89.9 us
    unnamed x14, local copies, waits for them, and re-layouts  6.64 us

profile of v2, /device:TPU:1, one launch (start us, length us, event | category | flops | bytes accessed | tf_op | source)
XLA Modules:
  0.0 97.2 jit_solution(10517273448501062835)
XLA Ops:
  0.0 0.0 copy-start
  0.0 1.6 %copy-done = f32[4,2,4,128,128]{4,3,2,1,0:T(8,128)S(1)} copy-done((f32[4,2,4,128,128]{4,3,2,1,0:T(8,128)S(1)}, f32[4,2,4,128,128]{4,3,2,1,0:T(8,128)}, u32[]{:S(2)}) %copy-start) | copy-done | bytes 2097176
  1.6 0.0 copy-start.1
  1.6 1.6 %copy-done.1 = f32[4,2,4,128,128]{4,3,2,1,0:T(8,128)S(1)} copy-done((f32[4,2,4,128,128]{4,3,2,1,0:T(8,128)S(1)}, f32[4,2,4,128,128]{4,3,2,1,0:T(8,128)}, u32[]{:S(2)}) %copy-start.1) | copy-done | bytes 2097176
  3.2 0.0 copy-start.2
  3.2 0.7 copy-done.2
  3.9 0.0 copy-start.3
  3.9 0.7 copy-done.3
  4.6 0.0 copy-start.4
  4.6 0.7 copy-done.4
  5.3 0.0 copy-start.5
  5.3 0.7 copy-done.5
  6.0 0.0 copy-start.6
  6.0 0.7 copy-done.6
  6.7 89.9 %shard_map.73 = f32[32,128]{1,0:T(8,128)S(1)} custom-call(f32[4,4,2,128]{3,2,1,0:T(2,128)S(1)} %copy-done.2, f32[4,2,4,128,128]{4,3,2,1,0:T(8,128)S(1)} %copy-done, f32[4,2,4,128,128]{4,3,2,1,0:T(8,128)S(1)} %copy-done.1, s32[4,2,4]{2,1,0:T(2,128)S(1)} %copy-done.3, s32[4,2,128]{2,1,0:T(2,128)S(1)} %copy-done.4, f32[4,2,128]{2,1,0:T(2,128)S(1)} %copy-done.5, ...), custom_call_target="tpu_custom_call" | custom-call | tf_op jit(solution)/shard_map/pallas_call | solution.py:370
  96.5 0.6 copy.10
Async XLA Ops:
  0.0 1.6 %copy-start = (f32[4,2,4,128,128]{4,3,2,1,0:T(8,128)S(1)}, f32[4,2,4,128,128]{4,3,2,1,0:T(8,128)}, u32[]{:S(2)}) copy-start(f32[4,2,4,128,128]{4,3,2,1,0:T(8,128)} %a_hbm.1) | copy-start | bytes 6291460
  1.6 1.6 %copy-start.1 = (f32[4,2,4,128,128]{4,3,2,1,0:T(8,128)S(1)}, f32[4,2,4,128,128]{4,3,2,1,0:T(8,128)}, u32[]{:S(2)}) copy-start(f32[4,2,4,128,128]{4,3,2,1,0:T(8,128)} %b_hbm.1) | copy-start | bytes 6291460
  3.2 0.7 copy-start.2
  3.9 0.7 copy-start.3
  4.6 0.7 copy-start.4
  5.3 0.7 copy-start.5
  6.0 0.7 copy-start.6

commit v3 on v2

--- a/solution.py
+++ b/solution.py
@@ -35,19 +35,6 @@
     gb = (nh // ga) * nd
     h = lax.axis_index("horiz")
     d = lax.axis_index("depth")
-
-    small = [
-        pltpu.make_async_copy(source, target, w_sem.at[2 + number])
-        for number, (source, target) in enumerate(
-            [(c_hbm, c_in), (upt_hbm, upt), (pat_hbm, pat), (mask_hbm, mask), (melt_hbm, melt)]
-        )
-    ]
-    for copy in small:
-        copy.start()
-    copy_a = pltpu.make_async_copy(a_hbm, st_a, w_sem.at[0])
-    copy_b = pltpu.make_async_copy(b_hbm, st_b, w_sem.at[1])
-    copy_a.start()
-    copy_b.start()
 
     h_hi = h // ga
     h_lo = lax.rem(h, ga)
@@ -75,27 +62,36 @@
         )
         sends.append((jnp.logical_and(in_h, in_d), (16 + src_h * 2) * 4, position * 4, n_rows, target))
 
-    def partner_a(k):
-        return (h_hi * ga + lax.rem(h_lo + k, ga), d)
-
-    def partner_b(k):
-        index = lax.rem(index_b + k, gb)
-        return ((index // nd) * ga + h_lo, lax.rem(index, nd))
+    nx = nh // ga
+    far = lambda k, n: min(k, n - k)
+    partners_a = [
+        (h_hi * ga + lax.rem(h_lo + k, ga), d)
+        for k in sorted(range(1, ga), key=lambda k: -far(k, ga))
+    ]
+    partners_b = [
+        (lax.rem(h_hi + i, nx) * ga + h_lo, lax.rem(d + j, nd))
+        for i, j in sorted(
+            [(i, j) for i in range(nx) for j in range(nd) if i + j],
+            key=lambda ij: -(far(ij[0], nx) + far(ij[1], nd)),
+        )
+    ]
 
     barrier = pltpu.get_barrier_semaphore()
-    for *_, target in sends:
+    for target in partners_a + partners_b + [target for *_, target in sends]:
         pl.semaphore_signal(barrier, inc=1, device_id=target, device_id_type=MESH)
 
-    def greet_a(k, _):
-        pl.semaphore_signal(barrier, inc=1, device_id=partner_a(k), device_id_type=MESH)
-        return 0
-
-    def greet_b(k, _):
-        pl.semaphore_signal(barrier, inc=1, device_id=partner_b(k), device_id_type=MESH)
-        return 0
-
-    lax.fori_loop(1, ga, greet_a, 0)
-    lax.fori_loop(1, gb, greet_b, 0)
+    small = [
+        pltpu.make_async_copy(source, target, w_sem.at[2 + number])
+        for number, (source, target) in enumerate(
+            [(c_hbm, c_in), (upt_hbm, upt), (pat_hbm, pat), (mask_hbm, mask), (melt_hbm, melt)]
+        )
+    ]
+    for copy in small:
+        copy.start()
+    copy_a = pltpu.make_async_copy(a_hbm, st_a, w_sem.at[0])
+    copy_b = pltpu.make_async_copy(b_hbm, st_b, w_sem.at[1])
+    copy_a.start()
+    copy_b.start()
 
     for copy in small:
         copy.wait()
@@ -147,10 +143,10 @@
     def split_blocks(stage, weights):
         def body(o, _):
             for k in range(4):
-                block = stage[o // 2, lax.rem(o, 2), k]
+                block = stage[o // 2, lax.rem(o, 2), k].T
                 high = block.astype(bf16)
-                weights[o, pl.ds(0, 128), pl.ds(k * 128, 128)] = high
-                weights[o, pl.ds(128, 128), pl.ds(k * 128, 128)] = (block - high.astype(f32)).astype(bf16)
+                weights[o, pl.ds(k * 128, 128), pl.ds(0, 128)] = high
+                weights[o, pl.ds(k * 128, 128), pl.ds(128, 128)] = (block - high.astype(f32)).astype(bf16)
             return 0
 
         lax.fori_loop(0, 8, body, 0)
@@ -175,7 +171,7 @@
                     axis=1,
                 )
                 both = lax.dot_general(
-                    lhs, weights[o], (((1,), (1,)), ((), ())), preferred_element_type=f32
+                    lhs, weights[o], (((1,), (0,)), ((), ())), preferred_element_type=f32
                 )
                 both = both[:, :128] + both[:, 128:]
                 sums.append(both + pltpu.roll(both, 4, axis=0))
@@ -185,28 +181,22 @@
     def all_sum(step, row):
         RA[step, h_lo] = row
 
-        def send_a(k, _):
+        for target in partners_a:
             pltpu.make_async_remote_copy(
                 src_ref=RA.at[step, h_lo], dst_ref=RA.at[step, h_lo],
                 send_sem=rs_sem.at[2 * step], recv_sem=ra_sem.at[step],
-                device_id=partner_a(k), device_id_type=MESH,
+                device_id=target, device_id_type=MESH,
             ).start()
-            return 0
-
-        lax.fori_loop(1, ga, send_a, 0)
         span = RA.at[step, pl.ds(0, ga - 1)]
         pltpu.make_async_copy(span, span, ra_sem.at[step]).wait()
         RB[step, index_b] = jnp.sum(RA[step], axis=0)
 
-        def send_b(k, _):
+        for target in partners_b:
             pltpu.make_async_remote_copy(
                 src_ref=RB.at[step, index_b], dst_ref=RB.at[step, index_b],
                 send_sem=rs_sem.at[2 * step + 1], recv_sem=rb_sem.at[step],
-                device_id=partner_b(k), device_id_type=MESH,
+                device_id=target, device_id_type=MESH,
             ).start()
-            return 0
-
-        lax.fori_loop(1, gb, send_b, 0)
         span = RB.at[step, pl.ds(0, gb - 1)]
         pltpu.make_async_copy(span, span, rb_sem.at[step]).wait()
         return jnp.sum(RB[step], axis=0)
@@ -383,8 +373,8 @@
             pltpu.SMEM((32,), jnp.int32),
             pltpu.VMEM((4, 2, 4, 128, 128), f32),
             pltpu.VMEM((4, 2, 4, 128, 128), f32),
-            pltpu.VMEM((8, 256, 512), bf16),
-            pltpu.VMEM((8, 256, 512), bf16),
+            pltpu.VMEM((8, 512, 256), bf16),
+            pltpu.VMEM((8, 512, 256), bf16),
             pltpu.VMEM((32, 128), f32),
             pltpu.VMEM((16, 128), f32),
             pltpu.VMEM((16, 8, 128), f32),
@@ -398,7 +388,7 @@
             pltpu.SemaphoreType.DMA((2 * NEWTON,)),
         ],
         compiler_params=pltpu.CompilerParams(
-            collective_id=0, has_side_effects=True, vmem_limit_bytes=24 * 1024 * 1024
+            collective_id=0, has_side_effects=True, vmem_limit_bytes=63 * 1024 * 1024
         ),
     )(state, explicit_blocks, implicit_blocks, pattern, cavity_mask, melt_rate, uptake_rate)
     return result.reshape(4, 2, 4, 128).transpose(2, 0, 1, 3)

time: 97.5 us -> 87.5 us (0.90)
  local copies, waits for them, and re-layouts: 7.26 us -> 1.33 us
  Pallas kernels: 89.9 us -> 85.9 us
    unnamed x14 -> x0, local copies, waits for them, and re-layouts: 6.64 us -> none
    pallas_call x1, Pallas kernels: 89.9 us -> 85.9 us  [per_device(): pl.pallas_call(functools.partial(kernel, nh, nd, ga), out_shape=jax.Shape...]
where the time goes in v3:
time: 87.5 us; the launch traced here: 87.3 us
  Pallas kernels  85.9 us (98%)
  local copies, waits for them, and re-layouts  1.33 us (2%)
    pallas_call x1, Pallas kernels, per_device(): pl.pallas_call(functools.partial(kernel, nh, nd, ga), out_shape=jax.Shape...  85.9 us

profile of v3, /device:TPU:1, one launch (start us, length us, event | category | flops | bytes accessed | tf_op | source)
XLA Modules:
  0.0 87.3 jit_solution(14858941916722928097)
XLA Ops:
  0.0 85.9 %shard_map.73 = f32[32,128]{1,0:T(8,128)} custom-call(f32[4,4,2,128]{3,2,1,0:T(2,128)} %c_hbm.1, f32[4,2,4,128,128]{4,3,2,1,0:T(8,128)} %a_hbm.1, f32[4,2,4,128,128]{4,3,2,1,0:T(8,128)} %b_hbm.1, s32[4,2,4]{2,1,0:T(2,128)} %pat_hbm.1, s32[4,2,128]{2,1,0:T(2,128)} %mask_hbm.1, f32[4,2,128]{2,1,0:T(2,128)} %melt_hbm.1, f32[4,2,128]{2,1,0:T(2,128)} %upt_hbm.1), custom_call_target="tpu_custom_call" | custom-call | tf_op jit(solution)/shard_map/pallas_call | solution.py:360
  85.9 1.3 %copy.10 = f32[4,2,4,128]{3,1,0,2:T(2,128)} copy(f32[4,2,4,128]{3,2,1,0:T(4,128)} %bitcast.4) | data formatting | bytes 32768 | tf_op jit(solution)/shard_map/reshape | solution.py:394

commit v4 on v3

--- a/solution.py
+++ b/solution.py
@@ -20,7 +20,7 @@
 SLOTS = 16
 ZERO = SLOTS * SLOT
 
-DIRECTIONS = [(1, 1), (-1, 1), (1, -1), (-1, -1), (0, 1), (0, -1), (1, 0), (-1, 0)]
+DIRECTIONS = [(1, 1), (1, -1), (1, 0), (0, 1), (0, -1), (-1, 1), (-1, -1), (-1, 0)]
 
 
 def rows(start, size):
@@ -30,7 +30,7 @@
 def kernel(
     nh, nd, ga, c_hbm, a_hbm, b_hbm, pat_hbm, mask_hbm, melt_hbm, upt_hbm, out,
     c_in, pat, mask, melt, upt, X, GB, IDX, st_a, st_b, WA, WB, PR, FU, K, RA, RB,
-    w_sem, r_sem, s_sem, ra_sem, rb_sem, rs_sem,
+    w_sem, r_sem, o_sem, s_sem, ra_sem, rb_sem, rs_sem,
 ):
     gb = (nh // ga) * nd
     h = lax.axis_index("horiz")
@@ -41,35 +41,38 @@
     index_b = h_hi * nd + d
 
     sends = []
-    for sh, sd in DIRECTIONS:
-        n_rows = 16 if sh else 32
-        src_h = {1: 4, -1: 2, 0: 2}[sh]
-        dst_h = {1: 0, -1: 6, 0: 2}[sh]
+    outward = 2 * lax.rem(h, 2) - 1
+    for side, sd in DIRECTIONS:
+        n_rows = 16 if side else 32
+        sh = side * outward
+        src_h = 3 + sh if side else 2
+        dst_h = 3 - 3 * sh if side else 2
         in_h = jnp.logical_and(h + sh >= 0, h + sh < nh)
         in_d = jnp.logical_and(d + sd >= 0, d + sd < nd)
         other_d = d + 1 - 2 * lax.rem(d, 2)
         other_h = h + 1 - 2 * lax.rem(h, 2)
-        near_h = h + sh if sh else other_h
+        near_h = h + sh if side else other_h
         target = (
             jnp.where(in_h, jnp.where(in_d, h + sh, near_h), h),
             jnp.where(in_h, jnp.where(in_d, d + sd, d), other_d),
         )
-        far_h = {1: 6, -1: 0, 0: 2}[sh]
+        far_h = 3 + 3 * sh if side else 2
         position = jnp.where(
             in_h,
             jnp.where(in_d, (1 - sd) * 16 + dst_h * 2, (1 + sd) * 16 + dst_h * 2),
             (1 - sd) * 16 + far_h * 2,
         )
-        sends.append((jnp.logical_and(in_h, in_d), (16 + src_h * 2) * 4, position * 4, n_rows, target))
+        sends.append((jnp.logical_and(in_h, in_d), (16 + src_h * 2) * 4, position * 4, n_rows, target, side == 1))
 
     nx = nh // ga
     far = lambda k, n: min(k, n - k)
+    other_lo = h_lo + 1 - 2 * lax.rem(h_lo, 2)
     partners_a = [
         (h_hi * ga + lax.rem(h_lo + k, ga), d)
         for k in sorted(range(1, ga), key=lambda k: -far(k, ga))
     ]
     partners_b = [
-        (lax.rem(h_hi + i, nx) * ga + h_lo, lax.rem(d + j, nd))
+        (lax.rem(h_hi + i, nx) * ga + other_lo, lax.rem(d + j, nd))
         for i, j in sorted(
             [(i, j) for i in range(nx) for j in range(nd) if i + j],
             key=lambda ij: -(far(ij[0], nx) + far(ij[1], nd)),
@@ -77,7 +80,8 @@
     ]
 
     barrier = pltpu.get_barrier_semaphore()
-    for target in partners_a + partners_b + [target for *_, target in sends]:
+    halo = [target for *_, target, _ in sends]
+    for target in partners_a[:3] + halo[:3] + partners_b[:5] + partners_a[3:7] + halo[3:] + partners_b[5:] + partners_a[7:]:
         pl.semaphore_signal(barrier, inc=1, device_id=target, device_id_type=MESH)
 
     small = [
@@ -119,18 +123,18 @@
 
     def exchange(slot):
         base = slot * SLOT
-        for inside, src, dst, n_rows, target in sends:
+        for inside, src, dst, n_rows, target, outer in sends:
             pltpu.make_async_remote_copy(
                 src_ref=X.at[rows(jnp.where(inside, base + src, ZERO), n_rows)],
                 dst_ref=X.at[rows(base + dst, n_rows)],
                 send_sem=s_sem.at[slot],
-                recv_sem=r_sem.at[slot],
+                recv_sem=(o_sem if outer else r_sem).at[slot],
                 device_id=target,
                 device_id_type=MESH,
             ).start()
 
-    def arrived(slot, sem):
-        span = X.at[rows(slot * SLOT, SLOT - 32)]
+    def finished(slot, sem, size):
+        span = X.at[rows(slot * SLOT, size)]
         pltpu.make_async_copy(span, span, sem.at[slot]).wait()
 
     def own(slot):
@@ -153,29 +157,42 @@
 
     upper = lax.broadcasted_iota(jnp.int32, (8, 128), 0) < 4
 
-    def product(slot, weights):
-        for pair in range(24):
-            x = X[pl.ds(pl.multiple_of(slot * SLOT + pair * 8, 8), 8), :]
-            high = x.astype(bf16).astype(f32)
-            low = pltpu.roll(x - high, 4, axis=0)
-            GB[2 * pair] = jnp.where(upper, high, low)
-            GB[2 * pair + 1] = jnp.where(upper, low, high)
-        for pair in range(4):
+    core = lax.rem(h, 2)
+    inner_rows = (1 - core) * 16
+    outer_rows = core * 48
+
+    def spread(slot, first, tiles):
+        for band in range(3):
+            for i in range(tiles):
+                row = band * 64 + first + i * 8
+                x = X[pl.ds(pl.multiple_of(slot * SLOT + row, 8), 8), :]
+                high = x.astype(bf16).astype(f32)
+                low = pltpu.roll(x - high, 4, axis=0)
+                place = lax.div(row, 4)
+                GB[place] = jnp.where(upper, high, low)
+                GB[place + 1] = jnp.where(upper, low, high)
+
+    def half_product(weights, first):
+        for pair in range(2):
             sums = []
-            for o in (2 * pair, 2 * pair + 1):
-                lhs = jnp.concatenate(
-                    [
-                        GB[IDX[o * 4 + k]].astype(bf16)
-                        for k in range(4)
-                    ],
-                    axis=1,
-                )
+            for o in (first + 2 * pair, first + 2 * pair + 1):
+                lhs = jnp.concatenate([GB[IDX[o * 4 + k]].astype(bf16) for k in range(4)], axis=1)
                 both = lax.dot_general(
                     lhs, weights[o], (((1,), (0,)), ((), ())), preferred_element_type=f32
                 )
                 both = both[:, :128] + both[:, 128:]
                 sums.append(both + pltpu.roll(both, 4, axis=0))
-            PR[pl.ds(pair * 8, 8), :] = jnp.where(upper, sums[0], sums[1])
+            PR[pl.ds(pl.multiple_of(first * 4 + pair * 8, 8), 8), :] = jnp.where(upper, sums[0], sums[1])
+
+    def product(slot, weights, remote=True):
+        if remote:
+            finished(slot, r_sem, 112)
+        spread(slot, inner_rows, 6)
+        half_product(weights, 4 * (1 - core))
+        if remote:
+            finished(slot, o_sem, 48)
+        spread(slot, outer_rows, 2)
+        half_product(weights, 4 * core)
         return [PR[pl.ds(t, 8, stride=4), :] for t in range(4)]
 
     def all_sum(step, row):
@@ -278,12 +295,10 @@
                 0.4 * v[2] + 0.25 * change,
                 0.5 * v[3] + 0.5 * forcing * v[0] - 0.025 * change,
             ]
-            arrived(slot, r_sem)
             image = product(slot, WA)
             middle = [m + i for m, i in zip(middle, image)]
             set_own(slot + 1, middle)
             exchange(slot + 1)
-            arrived(slot + 1, r_sem)
             image = product(slot + 1, WB)
             for t in range(4):
                 K[4 * (j + 1) + t] = middle[t] + image[t] - SHIFT * v[t]
@@ -295,7 +310,6 @@
     exchange(UPTAKE)
     copy_a.wait()
     split_blocks(st_a, WA)
-    arrived(0, r_sem)
     image = product(0, WA)
     c = own(0)
     forcing, uptake = FU[pl.ds(0, 8), :], FU[pl.ds(8, 8), :]
@@ -311,12 +325,12 @@
     exchange(1)
     copy_b.wait()
     split_blocks(st_b, WB)
-    arrived(1, r_sem)
     image = product(1, WB)
     krylov(2, c, [c[t] - middle[t] - image[t] for t in range(4)])
     weights = coefficients(0)
 
-    arrived(UPTAKE, r_sem)
+    finished(UPTAKE, r_sem, 112)
+    finished(UPTAKE, o_sem, 48)
 
     def wide(slot, t):
         return X[pl.ds(slot * SLOT + t, 48, stride=4), :]
@@ -335,7 +349,7 @@
         if t:
             value = value + (0.0, -0.5, 0.25, -0.025)[t] * rest
         X[pl.ds(8 * SLOT + t, 48, stride=4), :] = value
-    image = product(8, WB)
+    image = product(8, WB, remote=False)
     middle = own(8)
     c = [own(0)[t] + sum(weights[j] * K[4 * j + t] for j in range(3)) for t in range(4)]
 
@@ -345,7 +359,7 @@
         out[pl.ds(t, 8, stride=4), :] = c[t] + sum(weights[j] * K[4 * j + t] for j in range(3))
 
     for slot in (0, 1, 2, 3, 4, 5, 6, 7, 9, 10, 11, 12, 13, 14, UPTAKE):
-        arrived(slot, s_sem)
+        finished(slot, s_sem, 160)
     for step in range(NEWTON):
         span = RA.at[step, pl.ds(0, ga - 1)]
         pltpu.make_async_copy(span, span, rs_sem.at[2 * step]).wait()
@@ -383,6 +397,7 @@
             pltpu.SemaphoreType.DMA((7,)),
             pltpu.SemaphoreType.DMA((SLOTS,)),
             pltpu.SemaphoreType.DMA((SLOTS,)),
+            pltpu.SemaphoreType.DMA((SLOTS,)),
             pltpu.SemaphoreType.DMA((NEWTON,)),
             pltpu.SemaphoreType.DMA((NEWTON,)),
             pltpu.SemaphoreType.DMA((2 * NEWTON,)),

time: 87.5 us -> 85.5 us (0.977)
  Pallas kernels: 85.9 us -> 83.9 us
    pallas_call x1, Pallas kernels: 85.9 us -> 83.9 us  [per_device(): pl.pallas_call(functools.partial(kernel, nh, nd, ga), out_shape=jax.Shape...]
where the time goes in v4:
time: 85.5 us; the launch traced here: 85.3 us
  Pallas kernels  83.9 us (98%)
  local copies, waits for them, and re-layouts  1.33 us (2%)
    pallas_call x1, Pallas kernels, per_device(): pl.pallas_call(functools.partial(kernel, nh, nd, ga), out_shape=jax.Shape...  83.9 us

profile of v4, /device:TPU:1, one launch (start us, length us, event | category | flops | bytes accessed | tf_op | source)
XLA Modules:
  0.0 85.3 jit_solution(2064638105906420862)
XLA Ops:
  0.0 83.9 %shard_map.73 = f32[32,128]{1,0:T(8,128)} custom-call(f32[4,4,2,128]{3,2,1,0:T(2,128)} %c_hbm.1, f32[4,2,4,128,128]{4,3,2,1,0:T(8,128)} %a_hbm.1, f32[4,2,4,128,128]{4,3,2,1,0:T(8,128)} %b_hbm.1, s32[4,2,4]{2,1,0:T(2,128)} %pat_hbm.1, s32[4,2,128]{2,1,0:T(2,128)} %mask_hbm.1, f32[4,2,128]{2,1,0:T(2,128)} %melt_hbm.1, f32[4,2,128]{2,1,0:T(2,128)} %upt_hbm.1), custom_call_target="tpu_custom_call" | custom-call | tf_op jit(solution)/shard_map/pallas_call | solution.py:374
  83.9 1.3 %copy.10 = f32[4,2,4,128]{3,1,0,2:T(2,128)} copy(f32[4,2,4,128]{3,2,1,0:T(4,128)} %bitcast.4) | data formatting | bytes 32768 | tf_op jit(solution)/shard_map/reshape | solution.py:409

commit v5 on v4

--- a/solution.py
+++ b/solution.py
@@ -16,8 +16,9 @@
 
 SLOT = 192
 OWN = 80
-UPTAKE = 15
-SLOTS = 16
+CHANGED = 9
+UPTAKE = 17
+SLOTS = 18
 ZERO = SLOTS * SLOT
 
 DIRECTIONS = [(1, 1), (1, -1), (1, 0), (0, 1), (0, -1), (-1, 1), (-1, -1), (-1, 0)]
@@ -29,8 +30,8 @@
 
 def kernel(
     nh, nd, ga, c_hbm, a_hbm, b_hbm, pat_hbm, mask_hbm, melt_hbm, upt_hbm, out,
-    c_in, pat, mask, melt, upt, X, GB, IDX, st_a, st_b, WA, WB, PR, FU, K, RA, RB,
-    w_sem, r_sem, o_sem, s_sem, ra_sem, rb_sem, rs_sem,
+    c_in, pat, mask, melt, upt, X, GB, IDX, st_a, st_b, WA, WB, FU, RA, RB,
+    w_sem, r_sem, o_sem, s_sem, ra_sem, rb_sem, rs_sem, in_sem,
 ):
     gb = (nh // ga) * nd
     h = lax.axis_index("horiz")
@@ -79,9 +80,35 @@
         )
     ]
 
+    def ring(n, *offsets):
+        return sorted({k % n for k in offsets} - {0})
+
+    def along_z(*offsets):
+        return [(h_hi * ga + lax.rem(h_lo + k, ga), d) for k in ring(ga, *offsets)]
+
+    def along_x(*offsets):
+        return [(lax.rem(h_hi + k, nx) * ga + h_lo, d) for k in ring(nx, *offsets)]
+
+    def along_y(*offsets):
+        return [(h, lax.rem(d + k, nd)) for k in ring(nd, *offsets)]
+
+    nearest = along_z(1, -1) + along_x(1, -1) + along_y(1, -1)
+    rounds = [
+        nearest,
+        along_z(2, -2) + along_x(1, -1, 2),
+        along_z(4, -4) + [(h_hi * ga + other_lo, d)],
+    ]
+
+    def tell(number):
+        for target in rounds[number]:
+            pl.semaphore_signal(in_sem.at[number], inc=1, device_id=target, device_id_type=MESH)
+
+    def told(number):
+        pl.semaphore_wait(in_sem.at[number], len(rounds[number]))
+
     barrier = pltpu.get_barrier_semaphore()
-    halo = [target for *_, target, _ in sends]
-    for target in partners_a[:3] + halo[:3] + partners_b[:5] + partners_a[3:7] + halo[3:] + partners_b[5:] + partners_a[7:]:
+    greeted = [target for *_, target, _ in sends] + nearest
+    for target in greeted:
         pl.semaphore_signal(barrier, inc=1, device_id=target, device_id_type=MESH)
 
     small = [
@@ -119,7 +146,7 @@
             band = lax.div(dep, 2)
             IDX[o * 4 + k] = band * 16 + row * 2 + dep - 2 * band
 
-    pl.semaphore_wait(barrier, 8 + (ga - 1) + (gb - 1))
+    pl.semaphore_wait(barrier, len(greeted))
 
     def exchange(slot):
         base = slot * SLOT
@@ -140,6 +167,9 @@
     def own(slot):
         return [X[pl.ds(slot * SLOT + OWN + t, 8, stride=4), :] for t in range(4)]
 
+    def own_rows(slot):
+        return X[rows(slot * SLOT + OWN, 32), :]
+
     def set_own(slot, value):
         for t in range(4):
             X[pl.ds(slot * SLOT + OWN + t, 8, stride=4), :] = value[t]
@@ -172,7 +202,7 @@
                 GB[place] = jnp.where(upper, high, low)
                 GB[place + 1] = jnp.where(upper, low, high)
 
-    def half_product(weights, first):
+    def half_product(weights, first, target, sign):
         for pair in range(2):
             sums = []
             for o in (first + 2 * pair, first + 2 * pair + 1):
@@ -182,18 +212,19 @@
                 )
                 both = both[:, :128] + both[:, 128:]
                 sums.append(both + pltpu.roll(both, 4, axis=0))
-            PR[pl.ds(pl.multiple_of(first * 4 + pair * 8, 8), 8), :] = jnp.where(upper, sums[0], sums[1])
-
-    def product(slot, weights, remote=True):
+            image = jnp.where(upper, sums[0], sums[1])
+            place = pl.ds(pl.multiple_of(target * SLOT + OWN + first * 4 + pair * 8, 8), 8)
+            X[place, :] = X[place, :] + image if sign > 0 else X[place, :] - image
+
+    def product(slot, weights, target, sign=1, remote=True):
         if remote:
             finished(slot, r_sem, 112)
         spread(slot, inner_rows, 6)
-        half_product(weights, 4 * (1 - core))
+        half_product(weights, 4 * (1 - core), target, sign)
         if remote:
             finished(slot, o_sem, 48)
         spread(slot, outer_rows, 2)
-        half_product(weights, 4 * core)
-        return [PR[pl.ds(t, 8, stride=4), :] for t in range(4)]
+        half_product(weights, 4 * core, target, sign)
 
     def all_sum(step, row):
         RA[step, h_lo] = row
@@ -220,8 +251,8 @@
 
     lane = lax.broadcasted_iota(jnp.int32, (1, 128), 1)
 
-    def coefficients(step):
-        vectors = [[K[j * 4 + t] for t in range(4)] for j in range(4)]
+    def coefficients(step, first):
+        vectors = [[X[pl.ds((first + 2 * j) * SLOT + OWN + 8 * t, 8), :] for t in range(4)] for j in range(4)]
         pairs = [(i, j) for i in range(4) for j in range(i, 4)]
         row = jnp.zeros((1, 128), f32)
         for number, (i, j) in enumerate(pairs):
@@ -276,41 +307,37 @@
         denominator = 1.0 + iron * iron
         return 2.0 * iron / (denominator * denominator)
 
-    def krylov(first, c, residual):
+    def krylov(first, c):
         forcing, uptake = FU[pl.ds(0, 8), :], FU[pl.ds(8, 8), :]
         flux_one = uptake * limitation(c[3])
         flux_three = uptake * c[1] * slope(c[3])
-        for t in range(4):
-            K[t] = residual[t]
 
         def step(j, _):
-            v = [K[4 * j + t] for t in range(4)]
             slot = first + 2 * j
-            set_own(slot, v)
             exchange(slot)
+            v = own(slot)
             change = flux_one * v[1] + flux_three * v[3]
-            middle = [
-                0.5 * v[0] - 0.5 * forcing * v[0],
-                0.5 * v[1] - 0.5 * change,
-                0.4 * v[2] + 0.25 * change,
-                0.5 * v[3] + 0.5 * forcing * v[0] - 0.025 * change,
-            ]
-            image = product(slot, WA)
-            middle = [m + i for m, i in zip(middle, image)]
-            set_own(slot + 1, middle)
+            set_own(
+                slot + 1,
+                [
+                    0.5 * v[0] - 0.5 * forcing * v[0],
+                    0.5 * v[1] - 0.5 * change,
+                    0.4 * v[2] + 0.25 * change,
+                    0.5 * v[3] + 0.5 * forcing * v[0] - 0.025 * change,
+                ],
+            )
+            product(slot, WA, slot + 1)
             exchange(slot + 1)
-            image = product(slot + 1, WB)
-            for t in range(4):
-                K[4 * (j + 1) + t] = middle[t] + image[t] - SHIFT * v[t]
+            X[rows((slot + 2) * SLOT + OWN, 32), :] = own_rows(slot + 1) - SHIFT * own_rows(slot)
+            product(slot + 1, WB, slot + 2)
             return 0
 
         lax.fori_loop(0, KRYLOV, step, 0)
 
     exchange(0)
-    exchange(UPTAKE)
+    tell(0)
     copy_a.wait()
     split_blocks(st_a, WA)
-    image = product(0, WA)
     c = own(0)
     forcing, uptake = FU[pl.ds(0, 8), :], FU[pl.ds(8, 8), :]
     flux = uptake * c[1] * limitation(c[3])
@@ -320,14 +347,21 @@
         0.5 * flux - 0.2 * c[2],
         forcing * c[0] - 0.05 * flux,
     ]
-    middle = [0.5 * c[t] + image[t] + 0.5 * source[t] for t in range(4)]
-    set_own(1, middle)
+    set_own(1, [0.5 * c[t] + 0.5 * source[t] for t in range(4)])
+    product(0, WA, 1)
     exchange(1)
+    exchange(UPTAKE)
     copy_b.wait()
     split_blocks(st_b, WB)
-    image = product(1, WB)
-    krylov(2, c, [c[t] - middle[t] - image[t] for t in range(4)])
-    weights = coefficients(0)
+    told(0)
+    tell(1)
+    X[rows(2 * SLOT + OWN, 32), :] = own_rows(0) - own_rows(1)
+    product(1, WB, 2, sign=-1)
+    told(1)
+    tell(2)
+    krylov(2, c)
+    told(2)
+    weights = coefficients(0, 2)
 
     finished(UPTAKE, r_sem, 112)
     finished(UPTAKE, o_sem, 48)
@@ -348,17 +382,16 @@
         value = wide(1, t) + wide_sum(3, t)
         if t:
             value = value + (0.0, -0.5, 0.25, -0.025)[t] * rest
-        X[pl.ds(8 * SLOT + t, 48, stride=4), :] = value
-    image = product(8, WB, remote=False)
-    middle = own(8)
-    c = [own(0)[t] + sum(weights[j] * K[4 * j + t] for j in range(3)) for t in range(4)]
-
-    krylov(9, c, [c[t] - middle[t] - image[t] for t in range(4)])
-    weights = coefficients(1)
-    for t in range(4):
-        out[pl.ds(t, 8, stride=4), :] = c[t] + sum(weights[j] * K[4 * j + t] for j in range(3))
-
-    for slot in (0, 1, 2, 3, 4, 5, 6, 7, 9, 10, 11, 12, 13, 14, UPTAKE):
+        X[pl.ds(CHANGED * SLOT + t, 48, stride=4), :] = value
+    changed = own_rows(0) + sum(weights[j] * own_rows(2 + 2 * j) for j in range(3))
+    X[rows(10 * SLOT + OWN, 32), :] = changed - own_rows(CHANGED)
+    product(CHANGED, WB, 10, sign=-1, remote=False)
+
+    krylov(10, [own(0)[t] + sum(weights[j] * own(2 + 2 * j)[t] for j in range(3)) for t in range(4)])
+    weights = coefficients(1, 10)
+    out[...] = changed + sum(weights[j] * own_rows(10 + 2 * j) for j in range(3))
+
+    for slot in (0, 1, 2, 3, 4, 5, 6, 7, 10, 11, 12, 13, 14, 15, UPTAKE):
         finished(slot, s_sem, 160)
     for step in range(NEWTON):
         span = RA.at[step, pl.ds(0, ga - 1)]
@@ -389,9 +422,7 @@
             pltpu.VMEM((4, 2, 4, 128, 128), f32),
             pltpu.VMEM((8, 512, 256), bf16),
             pltpu.VMEM((8, 512, 256), bf16),
-            pltpu.VMEM((32, 128), f32),
             pltpu.VMEM((16, 128), f32),
-            pltpu.VMEM((16, 8, 128), f32),
             pltpu.VMEM((NEWTON, ga, 1, 128), f32),
             pltpu.VMEM((NEWTON, gb, 1, 128), f32),
             pltpu.SemaphoreType.DMA((7,)),
@@ -401,6 +432,7 @@
             pltpu.SemaphoreType.DMA((NEWTON,)),
             pltpu.SemaphoreType.DMA((NEWTON,)),
             pltpu.SemaphoreType.DMA((2 * NEWTON,)),
+            pltpu.SemaphoreType.REGULAR((3,)),
         ],
         compiler_params=pltpu.CompilerParams(
             collective_id=0, has_side_effects=True, vmem_limit_bytes=63 * 1024 * 1024

time: 85.5 us -> 84 us (0.982)
  Pallas kernels: 83.9 us -> 82.4 us
    pallas_call x1, Pallas kernels: 83.9 us -> 82.4 us  [per_device(): pl.pallas_call(functools.partial(kernel, nh, nd, ga), out_shape=jax.Shape...]
where the time goes in v5:
time: 84 us; the launch traced here: 83.8 us
  Pallas kernels  82.4 us (98%)
  local copies, waits for them, and re-layouts  1.33 us (2%)
    pallas_call x1, Pallas kernels, per_device(): pl.pallas_call(functools.partial(kernel, nh, nd, ga), out_shape=jax.Shape...  82.4 us

profile of v5, /device:TPU:1, one launch (start us, length us, event | category | flops | bytes accessed | tf_op | source)
XLA Modules:
  0.0 83.8 jit_solution(3881015803216054848)
XLA Ops:
  0.0 82.4 %shard_map.73 = f32[32,128]{1,0:T(8,128)} custom-call(f32[4,4,2,128]{3,2,1,0:T(2,128)} %c_hbm.1, f32[4,2,4,128,128]{4,3,2,1,0:T(8,128)} %a_hbm.1, f32[4,2,4,128,128]{4,3,2,1,0:T(8,128)} %b_hbm.1, s32[4,2,4]{2,1,0:T(2,128)} %pat_hbm.1, s32[4,2,128]{2,1,0:T(2,128)} %mask_hbm.1, f32[4,2,128]{2,1,0:T(2,128)} %melt_hbm.1, f32[4,2,128]{2,1,0:T(2,128)} %upt_hbm.1), custom_call_target="tpu_custom_call" | custom-call | tf_op jit(solution)/shard_map/pallas_call | solution.py:407
  82.4 1.3 %copy.10 = f32[4,2,4,128]{3,1,0,2:T(2,128)} copy(f32[4,2,4,128]{3,2,1,0:T(4,128)} %bitcast.4) | data formatting | bytes 32768 | tf_op jit(solution)/shard_map/reshape | solution.py:441

commit v6 on v5

--- a/solution.py
+++ b/solution.py
@@ -9,6 +9,7 @@
 NEWTON = 2
 KRYLOV = 3
 SHIFT = 0.3
+SCALE = 0.015625
 
 f32 = jnp.float32
 bf16 = jnp.bfloat16
@@ -214,7 +215,7 @@
                 sums.append(both + pltpu.roll(both, 4, axis=0))
             image = jnp.where(upper, sums[0], sums[1])
             place = pl.ds(pl.multiple_of(target * SLOT + OWN + first * 4 + pair * 8, 8), 8)
-            X[place, :] = X[place, :] + image if sign > 0 else X[place, :] - image
+            X[place, :] = X[place, :] + image if sign == 1 else X[place, :] + sign * image
 
     def product(slot, weights, target, sign=1, remote=True):
         if remote:
@@ -278,7 +279,7 @@
                 for m in range(i):
                     value = value - R[m][i] * R[m][j]
                 R[i][j] = value * inverse
-        hess = [[(SHIFT - 1.0) * R[i][j] + R[i][j + 1] for j in range(3)] for i in range(4)]
+        hess = [[(SHIFT - 1.0) * R[i][j] + R[i][j + 1] / SCALE for j in range(3)] for i in range(4)]
         target = [R[0][0], zero, zero, zero]
         for c in range(3):
             top, low = hess[c][c], hess[c + 1][c]
@@ -328,8 +329,8 @@
             )
             product(slot, WA, slot + 1)
             exchange(slot + 1)
-            X[rows((slot + 2) * SLOT + OWN, 32), :] = own_rows(slot + 1) - SHIFT * own_rows(slot)
-            product(slot + 1, WB, slot + 2)
+            X[rows((slot + 2) * SLOT + OWN, 32), :] = SCALE * (own_rows(slot + 1) - SHIFT * own_rows(slot))
+            product(slot + 1, WB, slot + 2, sign=SCALE)
             return 0
 
         lax.fori_loop(0, KRYLOV, step, 0)

time: 84 us -> 84 us (level)
  no operation moved by 1% of the time
where the time goes in v6:
time: 84 us; the launch traced here: 83.8 us
  Pallas kernels  82.4 us (98%)
  local copies, waits for them, and re-layouts  1.33 us (2%)
    pallas_call x1, Pallas kernels, per_device(): pl.pallas_call(functools.partial(kernel, nh, nd, ga), out_shape=jax.Shape...  82.4 us

profile of v6, /device:TPU:1, one launch (start us, length us, event | category | flops | bytes accessed | tf_op | source)
XLA Modules:
  0.0 83.8 jit_solution(14173842583069016935)
XLA Ops:
  0.0 82.4 %shard_map.73 = f32[32,128]{1,0:T(8,128)} custom-call(f32[4,4,2,128]{3,2,1,0:T(2,128)} %c_hbm.1, f32[4,2,4,128,128]{4,3,2,1,0:T(8,128)} %a_hbm.1, f32[4,2,4,128,128]{4,3,2,1,0:T(8,128)} %b_hbm.1, s32[4,2,4]{2,1,0:T(2,128)} %pat_hbm.1, s32[4,2,128]{2,1,0:T(2,128)} %mask_hbm.1, f32[4,2,128]{2,1,0:T(2,128)} %melt_hbm.1, f32[4,2,128]{2,1,0:T(2,128)} %upt_hbm.1), custom_call_target="tpu_custom_call" | custom-call | tf_op jit(solution)/shard_map/pallas_call | solution.py:408
  82.5 1.3 %copy.10 = f32[4,2,4,128]{3,1,0,2:T(2,128)} copy(f32[4,2,4,128]{3,2,1,0:T(4,128)} %bitcast.4) | data formatting | bytes 32768 | tf_op jit(solution)/shard_map/reshape | solution.py:442

commit v7 on v6

--- a/solution.py
+++ b/solution.py
@@ -69,16 +69,20 @@
     nx = nh // ga
     far = lambda k, n: min(k, n - k)
     other_lo = h_lo + 1 - 2 * lax.rem(h_lo, 2)
+    core = lax.rem(h, 2)
+    half = ga // 2
+    z = lax.div(h_lo, 2)
+    index_a = (h_hi * nd + d) * 2 + core
     partners_a = [
-        (h_hi * ga + lax.rem(h_lo + k, ga), d)
-        for k in sorted(range(1, ga), key=lambda k: -far(k, ga))
+        (lax.rem(h_hi + i, nx) * ga + (other_lo if flip else h_lo), lax.rem(d + j, nd))
+        for i, j, flip in sorted(
+            [(i, j, f) for i in range(nx) for j in range(nd) for f in (0, 1) if i + j + f],
+            key=lambda p: -(far(p[0], nx) + far(p[1], nd)) + 0.5 * p[2],
+        )
     ]
     partners_b = [
-        (lax.rem(h_hi + i, nx) * ga + other_lo, lax.rem(d + j, nd))
-        for i, j in sorted(
-            [(i, j) for i in range(nx) for j in range(nd) if i + j],
-            key=lambda ij: -(far(ij[0], nx) + far(ij[1], nd)),
-        )
+        (h_hi * ga + lax.rem(z + k, half) * 2 + 1 - core, d)
+        for k in sorted(range(1, half), key=lambda k: -far(k, half))
     ]
 
     def ring(n, *offsets):
@@ -188,7 +192,6 @@
 
     upper = lax.broadcasted_iota(jnp.int32, (8, 128), 0) < 4
 
-    core = lax.rem(h, 2)
     inner_rows = (1 - core) * 16
     outer_rows = core * 48
 
@@ -228,25 +231,25 @@
         half_product(weights, 4 * core, target, sign)
 
     def all_sum(step, row):
-        RA[step, h_lo] = row
+        RA[step, index_a] = row
 
         for target in partners_a:
             pltpu.make_async_remote_copy(
-                src_ref=RA.at[step, h_lo], dst_ref=RA.at[step, h_lo],
+                src_ref=RA.at[step, index_a], dst_ref=RA.at[step, index_a],
                 send_sem=rs_sem.at[2 * step], recv_sem=ra_sem.at[step],
                 device_id=target, device_id_type=MESH,
             ).start()
-        span = RA.at[step, pl.ds(0, ga - 1)]
+        span = RA.at[step, pl.ds(0, 2 * gb - 1)]
         pltpu.make_async_copy(span, span, ra_sem.at[step]).wait()
-        RB[step, index_b] = jnp.sum(RA[step], axis=0)
+        RB[step, z] = jnp.sum(RA[step], axis=0)
 
         for target in partners_b:
             pltpu.make_async_remote_copy(
-                src_ref=RB.at[step, index_b], dst_ref=RB.at[step, index_b],
+                src_ref=RB.at[step, z], dst_ref=RB.at[step, z],
                 send_sem=rs_sem.at[2 * step + 1], recv_sem=rb_sem.at[step],
                 device_id=target, device_id_type=MESH,
             ).start()
-        span = RB.at[step, pl.ds(0, gb - 1)]
+        span = RB.at[step, pl.ds(0, half - 1)]
         pltpu.make_async_copy(span, span, rb_sem.at[step]).wait()
         return jnp.sum(RB[step], axis=0)
 
@@ -395,9 +398,9 @@
     for slot in (0, 1, 2, 3, 4, 5, 6, 7, 10, 11, 12, 13, 14, 15, UPTAKE):
         finished(slot, s_sem, 160)
     for step in range(NEWTON):
-        span = RA.at[step, pl.ds(0, ga - 1)]
+        span = RA.at[step, pl.ds(0, 2 * gb - 1)]
         pltpu.make_async_copy(span, span, rs_sem.at[2 * step]).wait()
-        span = RB.at[step, pl.ds(0, gb - 1)]
+        span = RB.at[step, pl.ds(0, half - 1)]
         pltpu.make_async_copy(span, span, rs_sem.at[2 * step + 1]).wait()
 
 
@@ -424,8 +427,8 @@
             pltpu.VMEM((8, 512, 256), bf16),
             pltpu.VMEM((8, 512, 256), bf16),
             pltpu.VMEM((16, 128), f32),
-            pltpu.VMEM((NEWTON, ga, 1, 128), f32),
-            pltpu.VMEM((NEWTON, gb, 1, 128), f32),
+            pltpu.VMEM((NEWTON, 2 * gb, 1, 128), f32),
+            pltpu.VMEM((NEWTON, ga // 2, 1, 128), f32),
             pltpu.SemaphoreType.DMA((7,)),
             pltpu.SemaphoreType.DMA((SLOTS,)),
             pltpu.SemaphoreType.DMA((SLOTS,)),

time: 84 us -> 84 us (level)
  no operation moved by 1% of the time
where the time goes in v7:
time: 84 us; the launch traced here: 83.7 us
  Pallas kernels  82.4 us (98%)
  local copies, waits for them, and re-layouts  1.33 us (2%)
    pallas_call x1, Pallas kernels, per_device(): pl.pallas_call(functools.partial(kernel, nh, nd, ga), out_shape=jax.Shape...  82.4 us

profile of v7, /device:TPU:1, one launch (start us, length us, event | category | flops | bytes accessed | tf_op | source)
XLA Modules:
  0.0 83.7 jit_solution(17403645064657792512)
XLA Ops:
  0.0 82.4 %shard_map.73 = f32[32,128]{1,0:T(8,128)} custom-call(f32[4,4,2,128]{3,2,1,0:T(2,128)} %c_hbm.1, f32[4,2,4,128,128]{4,3,2,1,0:T(8,128)} %a_hbm.1, f32[4,2,4,128,128]{4,3,2,1,0:T(8,128)} %b_hbm.1, s32[4,2,4]{2,1,0:T(2,128)} %pat_hbm.1, s32[4,2,128]{2,1,0:T(2,128)} %mask_hbm.1, f32[4,2,128]{2,1,0:T(2,128)} %melt_hbm.1, f32[4,2,128]{2,1,0:T(2,128)} %upt_hbm.1), custom_call_target="tpu_custom_call" | custom-call | tf_op jit(solution)/shard_map/pallas_call | solution.py:411
  82.4 1.3 %copy.10 = f32[4,2,4,128]{3,1,0,2:T(2,128)} copy(f32[4,2,4,128]{3,2,1,0:T(4,128)} %bitcast.4) | data formatting | bytes 32768 | tf_op jit(solution)/shard_map/reshape | solution.py:445
